TPU v7x, 128 devices: a whole 4x4x4 slice. The times are simulated.
128 devices in a mesh: rows: 32 (over z, y, core), cols: 4 (over x).
Axes of the slice: x: 4, y: 4, z: 4, core: 2. Of those that a mesh axis runs over, the one named last changes fastest.
Arguments:
- basis: float32 [64, 262144], P('cols', 'rows'), may hold values from -450 to 450
- blocks: bfloat16 [1024, 4, 256, 256], P('rows'), may hold values from -16 to 1, as said below
- far_cols: int32 [1024], P('rows'), may hold values from 0 to 1023, as said below
Outputs:
- basis_out: float32 [64, 262144], P('cols', 'rows')
- ritz: float32 [64, 64], P(None, 'cols')
Inputs may be any that keep to these rules, and one draw needn't show every extreme that they name: Off-diagonal entries are positive; each diagonal entry of a diagonal block is minus the sum of the other entries of its row over the four blocks, rounded to bfloat16. `far_cols`: the block rows of one device name at most 2 far columns among the block rows of any one device; the block rows of some device are named by exactly 2 block rows of every device.
All inputs are finite; a program needn't handle non-finite values.
Results may differ from a plain program's by a relative error of at most 0.0036.
Values may be sent and summed in bfloat16 or wider, within the bound.
No kernel may reach another device: no remote copies, remote signals or barrier semaphores. Data moves between devices by JAX's collectives and lax.ppermute only.
A program may use at most 128 MiB of HBM per device.

v0:
```python
import jax
import jax.numpy as jnp
from jax import lax
from jax.sharding import PartitionSpec as P

ITERS = 4


def with_halo(block, sides, width):
    for axis, dim in sides:
        count = lax.axis_size(axis)
        forward = [(i, i + 1) for i in range(count - 1)]
        forward.append((count - 1, 0))
        backward = [(target, source) for source, target in forward]
        low = lax.ppermute(
            lax.slice_in_dim(block, block.shape[dim] - width, None, axis=dim), axis, forward
        )
        high = lax.ppermute(lax.slice_in_dim(block, 0, width, axis=dim), axis, backward)
        block = jnp.concatenate([low, block, high], axis=dim)
    return block


def block_product(pieces, blocks, position):
    return jnp.einsum(
        "jbt,bst->jbs", pieces, blocks[:, position], preferred_element_type=jnp.float32
    )


def body(basis, blocks, far_cols):
    width = basis.shape[0]
    block_rows = blocks.shape[0]
    block_size = blocks.shape[2]
    row_devices = lax.axis_size("rows")
    total_states = block_rows * block_size * row_devices
    modes = width * lax.axis_size("cols")
    highest = lax.Precision.HIGHEST

    def apply_generator(iterate_bf):
        shaped = iterate_bf.reshape(width, block_rows, block_size)
        result = block_product(shaped, blocks, 0)
        empty = jnp.zeros((width, block_rows, block_size), jnp.bfloat16)
        piece = lax.all_gather(shaped, "rows", axis=1, tiled=True)
        inside = jnp.logical_and(far_cols >= 0, far_cols < piece.shape[1])
        taken = jnp.take(piece, jnp.clip(far_cols, 0, piece.shape[1] - 1), axis=1)
        remote = jnp.where(inside[None, :, None], taken, empty)
        extended = with_halo(shaped, (("rows", 1),), 1)
        result = result + block_product(extended[:, :-2], blocks, 1)
        result = result + block_product(extended[:, 2:], blocks, 2)
        result = result + block_product(remote, blocks, 3)
        return result.reshape(width, block_rows * block_size)

    iterate = basis
    for step in range(ITERS):
        iterate = iterate + 0.2 * apply_generator(iterate.astype(jnp.bfloat16))
    whole_iterate = lax.all_gather(iterate, "cols", axis=0, tiled=True)
    contract = (((1,), (1,)), ((), ()))
    gram_part = lax.dot_general(whole_iterate, iterate, contract, precision=highest)
    column_start = lax.axis_index("cols") * width
    gram_mine = lax.psum(gram_part, "rows")
    gram = lax.all_gather(gram_mine, "cols", axis=1, tiled=True) / total_states
    applied = apply_generator(iterate.astype(jnp.bfloat16))
    product_part = lax.dot_general(whole_iterate, applied, contract, precision=highest)
    product_mine = lax.psum(product_part, "rows")
    product = lax.all_gather(product_mine, "cols", axis=1, tiled=True) / total_states
    factor = jnp.linalg.cholesky(gram)
    identity_square = jnp.eye(modes, dtype=factor.dtype)
    inverse_factor = lax.linalg.triangular_solve(
        factor, identity_square, left_side=True, lower=True
    )
    own_rows = lax.dynamic_slice_in_dim(inverse_factor, column_start, width, 0)
    basis_out = jnp.dot(own_rows, whole_iterate, precision=highest)
    left_part = jnp.dot(inverse_factor, product, precision=highest)
    ritz_whole = jnp.dot(left_part, inverse_factor.T, precision=highest)
    ritz = lax.dynamic_slice_in_dim(ritz_whole, column_start, width, 1)
    return (basis_out, ritz)


def solution(mesh):
    in_specs = (P("cols", "rows"), P("rows", None, None, None), P("rows"))
    out_specs = (P("cols", "rows"), P(None, "cols"))
    return jax.shard_map(body, mesh=mesh, in_specs=in_specs, out_specs=out_specs, check_vma=False)
```

profile of v0, /device:TPU:0, one launch (start us, length us, event | category | flops | bytes accessed | tf_op | source)
XLA Modules:
  0.0 539.1 jit_solution(13265493274930220181)
XLA Ops:
  9.8 6.0 %collective-permute-start.1 = (bf16[16,1,256]{2,0,1:T(8,128)(2,1)S(1)}, bf16[16,1,256]{2,0,1:T(8,128)(2,1)S(1)}, u32[]{:S(2)}, u32[]{:S(2)}) collective-permute-start(bf16[16,1,256]{2,0,1:T(8,128)(2,1)S(1)} %get-tuple-element.23), channel_id=1, source_target_pairs={{4,0},{8,4},{12,8},{16,12},{20,16},{24,20},{28,24},{32,28},{36,32}... | collective-permute-start | bytes 24584 | tf_op jit(solution)/shard_map/ppermute | solution.py:18
  19.9 3.6 fusion.84
  23.5 3.5 fusion.81
  27.0 39.3 %all-gather.7.cloned.1.call-done = bf16[16,1024,256]{2,0,1:T(8,128)(2,1)} async-done(((bf16[16,32,256]{2,0,1:T(8,128)(2,1)}), bf16[16,1024,256]{2,0,1:T(8,128)(2,1)}) %all-gather.7.cloned.1.call-update) | async-done | bytes 8388624 | tf_op jit(solution)/shard_map/all_gather | solution.py:42
  66.4 3.9 gather_fusion
  81.6 3.6 fusion.16
  85.2 42.1 %all-gather.9.cloned.1.call-done = bf16[16,1024,256]{2,0,1:T(8,128)(2,1)} async-done(((bf16[16,32,256]{2,0,1:T(8,128)(2,1)}), bf16[16,1024,256]{2,0,1:T(8,128)(2,1)}) %all-gather.9.cloned.1.call-update) | async-done | bytes 8388624 | tf_op jit(solution)/shard_map/all_gather | solution.py:42
  127.3 3.9 gather_fusion.1
  145.9 3.6 fusion.14
  149.6 42.1 %all-gather.11.cloned.1.call-done = bf16[16,1024,256]{2,0,1:T(8,128)(2,1)} async-done(((bf16[16,32,256]{2,0,1:T(8,128)(2,1)}), bf16[16,1024,256]{2,0,1:T(8,128)(2,1)}) %all-gather.11.cloned.1.call-update) | async-done | bytes 8388624 | tf_op jit(solution)/shard_map/all_gather | solution.py:42
  191.6 3.9 gather_fusion.2
  210.3 3.6 fusion.12
  213.9 42.1 %all-gather.13.cloned.1.call-done = bf16[16,1024,256]{2,0,1:T(8,128)(2,1)} async-done(((bf16[16,32,256]{2,0,1:T(8,128)(2,1)}), bf16[16,1024,256]{2,0,1:T(8,128)(2,1)}) %all-gather.13.cloned.1.call-update) | async-done | bytes 8388624 | tf_op jit(solution)/shard_map/all_gather | solution.py:42
  256.0 3.9 gather_fusion.3
  275.5 3.8 fusion.10
  279.3 18.8 %all-gather.15.cloned.1.call-done = f32[64,8192]{1,0:T(8,128)} async-done(((f32[16,8192]{1,0:T(8,128)}), f32[64,8192]{1,0:T(8,128)}) %all-gather.15.cloned.1.call-update) | async-done | bytes 2097168 | tf_op jit(solution)/shard_map/all_gather | solution.py:55
  301.5 51.9 %all-gather.17.cloned.1.call-done = bf16[16,1024,256]{2,0,1:T(8,128)(2,1)} async-done(((bf16[16,32,256]{2,0,1:T(8,128)(2,1)}), bf16[16,1024,256]{2,0,1:T(8,128)(2,1)}) %all-gather.17.cloned.1.call-update) | async-done | bytes 8388624 | tf_op jit(solution)/shard_map/all_gather | solution.py:42
  353.3 3.9 gather_fusion.4
  360.7 3.6 fusion.105
  366.1 126.6 %all-reduce = (f32[64,16]{0,1:T(8,128)S(1)}, f32[64,16]{0,1:T(8,128)S(1)}) all-reduce(f32[64,16]{0,1:T(8,128)S(1)} %fusion.239, f32[64,16]{0,1:T(8,128)S(1)} %fusion.240), channel_id=1, replica_groups=mesh['rows'=32,'cols'=4] {'rows'}, use_global_device_ids=true, to_apply=%region_0.2 | all-reduce | flops 2048 | bytes 16384 | tf_op jit(solution)/shard_map/psum | solution.py:59
  492.6 12.4 %all_gather.29 = f32[64,64]{0,1:T(8,128)S(1)} all-gather(f32[64,16]{0,1:T(8,128)S(1)} %get-tuple-element.3), channel_id=1, replica_groups=mesh['rows'=32,'cols'=4] {'cols'}, dimensions={1}, use_global_device_ids=true | all-gather | bytes 20480 | tf_op jit(solution)/shard_map/all_gather | solution.py:60
  505.2 5.8 %cholesky.17 = f32[64,64]{1,0:T(8,128)S(1)} custom-call(f32[64,64]{1,0:T(8,128)S(1)} %fusion.202), custom_call_target="Cholesky" | custom-call | tf_op jit(solution)/shard_map/jit(cholesky)/cholesky | solution.py:65
  512.4 4.9 custom-call.6
  517.5 11.9 %all_gather.31 = f32[64,64]{0,1:T(8,128)S(1)} all-gather(f32[64,16]{0,1:T(8,128)S(1)} %get-tuple-element.4), channel_id=1, replica_groups=mesh['rows'=32,'cols'=4] {'cols'}, dimensions={1}, use_global_device_ids=true | all-gather | bytes 20480 | tf_op jit(solution)/shard_map/all_gather | solution.py:64
  (95 shorter events, 75.7 us)
Async XLA Ops:
  7.2 59.2 %all-gather.7.cloned.1.call-start = ((), (), s32[]{:S(2)}) async-start(), calls=%async_computation | async-start | bytes 8650752 | tf_op jit(solution)/shard_map/all_gather | solution.py:42
  9.0 118.3 %all-gather.9.cloned.1.call-start = ((), (), s32[]{:S(2)}) async-start(), calls=%async_computation.1 | async-start | bytes 8650752 | tf_op jit(solution)/shard_map/all_gather | solution.py:42
  9.8 10.1 %collective-permute-start = (bf16[16,1,256]{2,0,1:T(8,128)(2,1)S(1)}, bf16[16,1,256]{2,0,1:T(8,128)(2,1)S(1)}, u32[]{:S(2)}, u32[]{:S(2)}) collective-permute-start(bf16[16,1,256]{2,0,1:T(8,128)(2,1)S(1)} %get-tuple-element.24), channel_id=1, source_target_pairs={{0,4},{4,8},{8,12},{12,16},{16,20},{20,24},{24,28},{28,32},{32,36}... | collective-permute-start | bytes 24584 | tf_op jit(solution)/shard_map/ppermute | solution.py:15
  9.8 13.7 %collective-permute-start.1 = (bf16[16,1,256]{2,0,1:T(8,128)(2,1)S(1)}, bf16[16,1,256]{2,0,1:T(8,128)(2,1)S(1)}, u32[]{:S(2)}, u32[]{:S(2)}) collective-permute-start(bf16[16,1,256]{2,0,1:T(8,128)(2,1)S(1)} %get-tuple-element.23), channel_id=1, source_target_pairs={{4,0},{8,4},{12,8},{16,12},{20,16},{24,20},{28,24},{32,28},{36,32}... | collective-permute-start | bytes 24584 | tf_op jit(solution)/shard_map/ppermute | solution.py:18
  19.9 3.6 copy-start.4
  23.5 50.3 %copy-start.2 = (f32[16,8192]{1,0:T(8,128)S(1)}, f32[16,8192]{1,0:T(8,128)}, u32[]{:S(2)}) copy-start(f32[16,8192]{1,0:T(8,128)} %param.5) | copy-start | bytes 1572868
  74.6 117.0 %all-gather.11.cloned.1.call-start = ((), (), s32[]{:S(2)}) async-start(), calls=%async_computation.2 | async-start | bytes 8650752 | tf_op jit(solution)/shard_map/all_gather | solution.py:42
  75.4 6.2 %collective-permute-start.3 = (bf16[16,1,256]{2,0,1:T(8,128)(2,1)S(1)}, bf16[16,1,256]{2,0,1:T(8,128)(2,1)S(1)}, u32[]{:S(2)}, u32[]{:S(2)}) collective-permute-start(bf16[16,1,256]{2,0,1:T(8,128)(2,1)S(1)} %get-tuple-element.22), channel_id=1, source_target_pairs={{4,0},{8,4},{12,8},{16,12},{20,16},{24,20},{28,24},{32,28},{36,32}... | collective-permute-start | bytes 24584 | tf_op jit(solution)/shard_map/ppermute | solution.py:18
  81.6 53.1 %copy-start.5 = (bf16[2,32,8,256]{3,2,0,1:T(8,128)(2,1)S(1)}, bf16[2,32,8,256]{3,2,0,1:T(8,128)(2,1)}, u32[]{:S(2)}) copy-start(bf16[2,32,8,256]{3,2,0,1:T(8,128)(2,1)} %copy.157) | copy-start | bytes 786436
  81.6 53.1 %collective-permute-start.2 = (bf16[16,1,256]{2,0,1:T(8,128)(2,1)S(1)}, bf16[16,1,256]{2,0,1:T(8,128)(2,1)S(1)}, u32[]{:S(2)}, u32[]{:S(2)}) collective-permute-start(bf16[16,1,256]{2,0,1:T(8,128)(2,1)S(1)} %get-tuple-element.21), channel_id=1, source_target_pairs={{0,4},{4,8},{8,12},{12,16},{16,20},{20,24},{24,28},{28,32},{32,36}... | collective-permute-start | bytes 24584 | tf_op jit(solution)/shard_map/ppermute | solution.py:15
  138.9 117.0 %all-gather.13.cloned.1.call-start = ((), (), s32[]{:S(2)}) async-start(), calls=%async_computation.3 | async-start | bytes 8650752 | tf_op jit(solution)/shard_map/all_gather | solution.py:42
  139.7 6.2 %collective-permute-start.5 = (bf16[16,1,256]{2,0,1:T(8,128)(2,1)S(1)}, bf16[16,1,256]{2,0,1:T(8,128)(2,1)S(1)}, u32[]{:S(2)}, u32[]{:S(2)}) collective-permute-start(bf16[16,1,256]{2,0,1:T(8,128)(2,1)S(1)} %get-tuple-element.20), channel_id=1, source_target_pairs={{4,0},{8,4},{12,8},{16,12},{20,16},{24,20},{28,24},{32,28},{36,32}... | collective-permute-start | bytes 24584 | tf_op jit(solution)/shard_map/ppermute | solution.py:18
  145.9 53.1 %copy-start.6 = (bf16[2,32,8,256]{3,2,0,1:T(8,128)(2,1)S(1)}, bf16[2,32,8,256]{3,2,0,1:T(8,128)(2,1)}, u32[]{:S(2)}) copy-start(bf16[2,32,8,256]{3,2,0,1:T(8,128)(2,1)} %copy.156) | copy-start | bytes 786436
  145.9 53.1 %collective-permute-start.4 = (bf16[16,1,256]{2,0,1:T(8,128)(2,1)S(1)}, bf16[16,1,256]{2,0,1:T(8,128)(2,1)S(1)}, u32[]{:S(2)}, u32[]{:S(2)}) collective-permute-start(bf16[16,1,256]{2,0,1:T(8,128)(2,1)S(1)} %get-tuple-element.19), channel_id=1, source_target_pairs={{0,4},{4,8},{8,12},{12,16},{16,20},{20,24},{24,28},{28,32},{32,36}... | collective-permute-start | bytes 24584 | tf_op jit(solution)/shard_map/ppermute | solution.py:15
  203.3 94.9 %all-gather.15.cloned.1.call-start = ((), (), s32[]{:S(2)}) async-start(), calls=%async_computation.4 | async-start | bytes 2621440 | tf_op jit(solution)/shard_map/all_gather | solution.py:55
  204.0 6.2 %collective-permute-start.7 = (bf16[16,1,256]{2,0,1:T(8,128)(2,1)S(1)}, bf16[16,1,256]{2,0,1:T(8,128)(2,1)S(1)}, u32[]{:S(2)}, u32[]{:S(2)}) collective-permute-start(bf16[16,1,256]{2,0,1:T(8,128)(2,1)S(1)} %get-tuple-element.18), channel_id=1, source_target_pairs={{4,0},{8,4},{12,8},{16,12},{20,16},{24,20},{28,24},{32,28},{36,32}... | collective-permute-start | bytes 24584 | tf_op jit(solution)/shard_map/ppermute | solution.py:18
  210.3 53.1 %copy-start.7 = (bf16[2,32,8,256]{3,2,0,1:T(8,128)(2,1)S(1)}, bf16[2,32,8,256]{3,2,0,1:T(8,128)(2,1)}, u32[]{:S(2)}) copy-start(bf16[2,32,8,256]{3,2,0,1:T(8,128)(2,1)} %copy.155) | copy-start | bytes 786436
  210.3 53.1 %collective-permute-start.6 = (bf16[16,1,256]{2,0,1:T(8,128)(2,1)S(1)}, bf16[16,1,256]{2,0,1:T(8,128)(2,1)S(1)}, u32[]{:S(2)}, u32[]{:S(2)}) collective-permute-start(bf16[16,1,256]{2,0,1:T(8,128)(2,1)S(1)} %get-tuple-element.17), channel_id=1, source_target_pairs={{0,4},{4,8},{8,12},{12,16},{16,20},{20,24},{24,28},{28,32},{32,36}... | collective-permute-start | bytes 24584 | tf_op jit(solution)/shard_map/ppermute | solution.py:15
  267.7 85.7 %all-gather.17.cloned.1.call-start = ((), (), s32[]{:S(2)}) async-start(), calls=%async_computation.5 | async-start | bytes 8650752 | tf_op jit(solution)/shard_map/all_gather | solution.py:42
  269.2 6.2 %collective-permute-start.9 = (bf16[16,1,256]{2,0,1:T(8,128)(2,1)S(1)}, bf16[16,1,256]{2,0,1:T(8,128)(2,1)S(1)}, u32[]{:S(2)}, u32[]{:S(2)}) collective-permute-start(bf16[16,1,256]{2,0,1:T(8,128)(2,1)S(1)} %get-tuple-element.16), channel_id=1, source_target_pairs={{4,0},{8,4},{12,8},{16,12},{20,16},{24,20},{28,24},{32,28},{36,32}... | collective-permute-start | bytes 24584 | tf_op jit(solution)/shard_map/ppermute | solution.py:18
  275.4 22.7 %copy-start.1 = (f32[16,8192]{1,0:T(8,128)S(1)}, f32[16,8192]{1,0:T(8,128)}, u32[]{:S(2)}) copy-start(f32[16,8192]{1,0:T(8,128)} %get-tuple-element.6) | copy-start | bytes 1572868
  275.4 85.3 %copy-start.3 = (bf16[2,32,8,256]{3,2,0,1:T(8,128)(2,1)S(1)}, bf16[2,32,8,256]{3,2,0,1:T(8,128)(2,1)}, u32[]{:S(2)}) copy-start(bf16[2,32,8,256]{3,2,0,1:T(8,128)(2,1)} %copy.154) | copy-start | bytes 786436
  275.4 85.3 %collective-permute-start.8 = (bf16[16,1,256]{2,0,1:T(8,128)(2,1)S(1)}, bf16[16,1,256]{2,0,1:T(8,128)(2,1)S(1)}, u32[]{:S(2)}, u32[]{:S(2)}) collective-permute-start(bf16[16,1,256]{2,0,1:T(8,128)(2,1)S(1)} %get-tuple-element.15), channel_id=1, source_target_pairs={{0,4},{4,8},{8,12},{12,16},{16,20},{20,24},{24,28},{28,32},{32,36}... | collective-permute-start | bytes 24584 | tf_op jit(solution)/shard_map/ppermute | solution.py:15
  360.7 3.6 copy-start
Sparse Core Ops, SparseCore 0:
  10.8 55.4 all-gather.6
  74.7 52.5 all-gather.8
  139.1 52.5 all-gather.10
  203.4 52.5 all-gather.12
  267.8 30.2 all-gather.14
  300.2 53.0 all-gather.16
where the time goes:
time: 540 us; the launch traced here: 539 us
  waiting for transfers between devices  236 us (44%)
  blocking collectives  151 us (28%)
  matrix products  77.1 us (14%)
  local copies, waits for them, and re-layouts  27.9 us (5%)
  starting transfers between devices  17.6 us (3%)
  other arithmetic  14.9 us (3%)
  between operations  14.4 us (3%)
    all_gather x5, waiting for transfers between devices, apply_generator(): piece = lax.all_gather(shaped, 'rows', axis=1, tiled=True)  217 us
    psum x1, blocking collectives, body(): gram_mine = lax.psum(gram_part, 'rows')  127 us
    dot_general x20, matrix products, block_product(): jnp.einsum('jbt,bst->jbs', pieces, blocks[:, position], preferred_element...  69.5 us
    gather x5, local copies, waits for them, and re-layouts, apply_generator(): taken = jnp.take(piece, jnp.clip(far_cols, 0, piece.shape[1] - 1), axis=1)  19.7 us
    all_gather x1, waiting for transfers between devices, body(): whole_iterate = lax.all_gather(iterate, 'cols', axis=0, tiled=True)  18.8 us
    ppermute x5, starting transfers between devices, with_halo(): lax.ppermute(lax.slice_in_dim(block, 0, width, axis=dim), axis, backward)  17.3 us
    all_gather x1, blocking collectives, body(): gram = lax.all_gather(gram_mine, 'cols', axis=1, tiled=True) / total_states  12.4 us
    all_gather x1, blocking collectives, body(): lax.all_gather(product_mine, 'cols', axis=1, tiled=True) / total_states  11.9 us
  transfers between devices with their start and end apart: 16, of which 6 were waited for; matrix products, arithmetic and copies ran while one was open for 14% of the time, Pallas kernels for 0%

commit v1 on v0

--- a/solution.py
+++ b/solution.py
@@ -57,7 +57,12 @@
     gram_part = lax.dot_general(whole_iterate, iterate, contract, precision=highest)
     column_start = lax.axis_index("cols") * width
     gram_mine = lax.psum(gram_part, "rows")
-    gram = lax.all_gather(gram_mine, "cols", axis=1, tiled=True) / total_states
+    gram = (
+        jnp.concatenate(
+            lax.all_to_all(jnp.stack([gram_mine] * lax.axis_size("cols")), "cols", 0, 0), axis=1
+        )
+        / total_states
+    )
     applied = apply_generator(iterate.astype(jnp.bfloat16))
     product_part = lax.dot_general(whole_iterate, applied, contract, precision=highest)
     product_mine = lax.psum(product_part, "rows")

time: 540 us -> 535 us (level)
  blocking collectives: 151 us -> 140 us
    all_gather x1 -> x0, blocking collectives: 12.4 us -> none  [body(): gram = lax.all_gather(gram_mine, 'cols', axis=1, tiled=True) / total_states]
  transfers between devices with their start and end apart: 16 -> 17, of which waited for: 6 -> 6; matrix products, arithmetic and copies ran while one was open for 14% -> 14% of each run, Pallas kernels for 0% -> 0%
where the time goes in v1:
time: 535 us; the launch traced here: 534 us
  waiting for transfers between devices  236 us (44%)
  blocking collectives  140 us (26%)
  matrix products  77.1 us (14%)
  local copies, waits for them, and re-layouts  29.2 us (5%)
  starting transfers between devices  21.8 us (4%)
  other arithmetic  15.6 us (3%)
  between operations  14.4 us (3%)
    all_gather x5, waiting for transfers between devices, apply_generator(): piece = lax.all_gather(shaped, 'rows', axis=1, tiled=True)  217 us
    psum x1, blocking collectives, body(): gram_mine = lax.psum(gram_part, 'rows')  127 us
    dot_general x20, matrix products, block_product(): jnp.einsum('jbt,bst->jbs', pieces, blocks[:, position], preferred_element...  69.5 us
    gather x5, local copies, waits for them, and re-layouts, apply_generator(): taken = jnp.take(piece, jnp.clip(far_cols, 0, piece.shape[1] - 1), axis=1)  19.7 us
    all_gather x1, waiting for transfers between devices, body(): whole_iterate = lax.all_gather(iterate, 'cols', axis=0, tiled=True)  18.8 us
    ppermute x5, starting transfers between devices, with_halo(): lax.ppermute(lax.slice_in_dim(block, 0, width, axis=dim), axis, backward)  17.3 us
    all_gather x1, blocking collectives, body(): lax.all_gather(product_mine, 'cols', axis=1, tiled=True) / total_states  13 us
  transfers between devices with their start and end apart: 17, of which 6 were waited for; matrix products, arithmetic and copies ran while one was open for 14% of the time, Pallas kernels for 0%

profile of v1, /device:TPU:0, one launch (start us, length us, event | category | flops | bytes accessed | tf_op | source)
XLA Modules:
  0.0 534.0 jit_solution(4215045404753814674)
XLA Ops:
  9.8 6.0 %collective-permute-start.1 = (bf16[16,1,256]{2,0,1:T(8,128)(2,1)S(1)}, bf16[16,1,256]{2,0,1:T(8,128)(2,1)S(1)}, u32[]{:S(2)}, u32[]{:S(2)}) collective-permute-start(bf16[16,1,256]{2,0,1:T(8,128)(2,1)S(1)} %get-tuple-element.23), channel_id=1, source_target_pairs={{4,0},{8,4},{12,8},{16,12},{20,16},{24,20},{28,24},{32,28},{36,32}... | collective-permute-start | bytes 24584 | tf_op jit(solution)/shard_map/ppermute | solution.py:18
  19.9 3.6 fusion.84
  23.5 3.5 fusion.81
  27.0 39.3 %all-gather.7.cloned.1.call-done = bf16[16,1024,256]{2,0,1:T(8,128)(2,1)} async-done(((bf16[16,32,256]{2,0,1:T(8,128)(2,1)}), bf16[16,1024,256]{2,0,1:T(8,128)(2,1)}) %all-gather.7.cloned.1.call-update) | async-done | bytes 8388624 | tf_op jit(solution)/shard_map/all_gather | solution.py:42
  66.4 3.9 gather_fusion
  81.6 3.6 fusion.16
  85.2 42.1 %all-gather.9.cloned.1.call-done = bf16[16,1024,256]{2,0,1:T(8,128)(2,1)} async-done(((bf16[16,32,256]{2,0,1:T(8,128)(2,1)}), bf16[16,1024,256]{2,0,1:T(8,128)(2,1)}) %all-gather.9.cloned.1.call-update) | async-done | bytes 8388624 | tf_op jit(solution)/shard_map/all_gather | solution.py:42
  127.3 3.9 gather_fusion.1
  146.0 3.6 fusion.14
  149.6 42.1 %all-gather.11.cloned.1.call-done = bf16[16,1024,256]{2,0,1:T(8,128)(2,1)} async-done(((bf16[16,32,256]{2,0,1:T(8,128)(2,1)}), bf16[16,1024,256]{2,0,1:T(8,128)(2,1)}) %all-gather.11.cloned.1.call-update) | async-done | bytes 8388624 | tf_op jit(solution)/shard_map/all_gather | solution.py:42
  191.6 3.9 gather_fusion.2
  210.3 3.6 fusion.12
  213.9 42.1 %all-gather.13.cloned.1.call-done = bf16[16,1024,256]{2,0,1:T(8,128)(2,1)} async-done(((bf16[16,32,256]{2,0,1:T(8,128)(2,1)}), bf16[16,1024,256]{2,0,1:T(8,128)(2,1)}) %all-gather.13.cloned.1.call-update) | async-done | bytes 8388624 | tf_op jit(solution)/shard_map/all_gather | solution.py:42
  256.0 3.9 gather_fusion.3
  275.5 3.8 fusion.10
  279.3 18.8 %all-gather.15.cloned.1.call-done = f32[64,8192]{1,0:T(8,128)} async-done(((f32[16,8192]{1,0:T(8,128)}), f32[64,8192]{1,0:T(8,128)}) %all-gather.15.cloned.1.call-update) | async-done | bytes 2097168 | tf_op jit(solution)/shard_map/all_gather | solution.py:55
  301.5 51.9 %all-gather.17.cloned.1.call-done = bf16[16,1024,256]{2,0,1:T(8,128)(2,1)} async-done(((bf16[16,32,256]{2,0,1:T(8,128)(2,1)}), bf16[16,1024,256]{2,0,1:T(8,128)(2,1)}) %all-gather.17.cloned.1.call-update) | async-done | bytes 8388624 | tf_op jit(solution)/shard_map/all_gather | solution.py:42
  353.4 3.9 gather_fusion.4
  360.8 3.5 fusion.105
  366.1 126.6 %all-reduce = (f32[64,16]{0,1:T(8,128)S(1)}, f32[64,16]{0,1:T(8,128)S(1)}) all-reduce(f32[64,16]{0,1:T(8,128)S(1)} %fusion.239, f32[64,16]{0,1:T(8,128)S(1)} %fusion.240), channel_id=1, replica_groups=mesh['rows'=32,'cols'=4] {'rows'}, use_global_device_ids=true, to_apply=%region_0.2 | all-reduce | flops 2048 | bytes 16384 | tf_op jit(solution)/shard_map/psum | solution.py:59
  493.4 4.2 all-to-all-start
  497.6 13.0 %all_gather.27 = f32[64,64]{0,1:T(8,128)S(1)} all-gather(f32[64,16]{0,1:T(8,128)S(1)} %get-tuple-element.4), channel_id=1, replica_groups=mesh['rows'=32,'cols'=4] {'cols'}, dimensions={1}, use_global_device_ids=true | all-gather | bytes 20480 | tf_op jit(solution)/shard_map/all_gather | solution.py:69
  512.0 5.8 %cholesky.17 = f32[64,64]{1,0:T(8,128)S(1)} custom-call(f32[64,64]{1,0:T(8,128)S(1)} %fusion.200), custom_call_target="Cholesky" | custom-call | tf_op jit(solution)/shard_map/jit(cholesky)/cholesky | solution.py:70
  519.2 4.9 custom-call.6
  (101 shorter events, 77.7 us)
Async XLA Ops:
  7.2 59.2 %all-gather.7.cloned.1.call-start = ((), (), s32[]{:S(2)}) async-start(), calls=%async_computation.1 | async-start | bytes 8650752 | tf_op jit(solution)/shard_map/all_gather | solution.py:42
  9.0 118.3 %all-gather.9.cloned.1.call-start = ((), (), s32[]{:S(2)}) async-start(), calls=%async_computation.2 | async-start | bytes 8650752 | tf_op jit(solution)/shard_map/all_gather | solution.py:42
  9.8 10.1 %collective-permute-start = (bf16[16,1,256]{2,0,1:T(8,128)(2,1)S(1)}, bf16[16,1,256]{2,0,1:T(8,128)(2,1)S(1)}, u32[]{:S(2)}, u32[]{:S(2)}) collective-permute-start(bf16[16,1,256]{2,0,1:T(8,128)(2,1)S(1)} %get-tuple-element.24), channel_id=1, source_target_pairs={{0,4},{4,8},{8,12},{12,16},{16,20},{20,24},{24,28},{28,32},{32,36}... | collective-permute-start | bytes 24584 | tf_op jit(solution)/shard_map/ppermute | solution.py:15
  9.8 13.7 %collective-permute-start.1 = (bf16[16,1,256]{2,0,1:T(8,128)(2,1)S(1)}, bf16[16,1,256]{2,0,1:T(8,128)(2,1)S(1)}, u32[]{:S(2)}, u32[]{:S(2)}) collective-permute-start(bf16[16,1,256]{2,0,1:T(8,128)(2,1)S(1)} %get-tuple-element.23), channel_id=1, source_target_pairs={{4,0},{8,4},{12,8},{16,12},{20,16},{24,20},{28,24},{32,28},{36,32}... | collective-permute-start | bytes 24584 | tf_op jit(solution)/shard_map/ppermute | solution.py:18
  23.5 50.3 %copy-start.2 = (f32[16,8192]{1,0:T(8,128)S(1)}, f32[16,8192]{1,0:T(8,128)}, u32[]{:S(2)}) copy-start(f32[16,8192]{1,0:T(8,128)} %param.5) | copy-start | bytes 1572868
  74.6 117.0 %all-gather.11.cloned.1.call-start = ((), (), s32[]{:S(2)}) async-start(), calls=%async_computation.3 | async-start | bytes 8650752 | tf_op jit(solution)/shard_map/all_gather | solution.py:42
  75.4 6.2 %collective-permute-start.3 = (bf16[16,1,256]{2,0,1:T(8,128)(2,1)S(1)}, bf16[16,1,256]{2,0,1:T(8,128)(2,1)S(1)}, u32[]{:S(2)}, u32[]{:S(2)}) collective-permute-start(bf16[16,1,256]{2,0,1:T(8,128)(2,1)S(1)} %get-tuple-element.22), channel_id=1, source_target_pairs={{4,0},{8,4},{12,8},{16,12},{20,16},{24,20},{28,24},{32,28},{36,32}... | collective-permute-start | bytes 24584 | tf_op jit(solution)/shard_map/ppermute | solution.py:18
  81.6 53.1 %copy-start.5 = (bf16[2,32,8,256]{3,2,0,1:T(8,128)(2,1)S(1)}, bf16[2,32,8,256]{3,2,0,1:T(8,128)(2,1)}, u32[]{:S(2)}) copy-start(bf16[2,32,8,256]{3,2,0,1:T(8,128)(2,1)} %copy.157) | copy-start | bytes 786436
  81.6 53.1 %collective-permute-start.2 = (bf16[16,1,256]{2,0,1:T(8,128)(2,1)S(1)}, bf16[16,1,256]{2,0,1:T(8,128)(2,1)S(1)}, u32[]{:S(2)}, u32[]{:S(2)}) collective-permute-start(bf16[16,1,256]{2,0,1:T(8,128)(2,1)S(1)} %get-tuple-element.21), channel_id=1, source_target_pairs={{0,4},{4,8},{8,12},{12,16},{16,20},{20,24},{24,28},{28,32},{32,36}... | collective-permute-start | bytes 24584 | tf_op jit(solution)/shard_map/ppermute | solution.py:15
  139.0 117.0 %all-gather.13.cloned.1.call-start = ((), (), s32[]{:S(2)}) async-start(), calls=%async_computation.4 | async-start | bytes 8650752 | tf_op jit(solution)/shard_map/all_gather | solution.py:42
  139.7 6.2 %collective-permute-start.5 = (bf16[16,1,256]{2,0,1:T(8,128)(2,1)S(1)}, bf16[16,1,256]{2,0,1:T(8,128)(2,1)S(1)}, u32[]{:S(2)}, u32[]{:S(2)}) collective-permute-start(bf16[16,1,256]{2,0,1:T(8,128)(2,1)S(1)} %get-tuple-element.20), channel_id=1, source_target_pairs={{4,0},{8,4},{12,8},{16,12},{20,16},{24,20},{28,24},{32,28},{36,32}... | collective-permute-start | bytes 24584 | tf_op jit(solution)/shard_map/ppermute | solution.py:18
  145.9 53.1 %copy-start.6 = (bf16[2,32,8,256]{3,2,0,1:T(8,128)(2,1)S(1)}, bf16[2,32,8,256]{3,2,0,1:T(8,128)(2,1)}, u32[]{:S(2)}) copy-start(bf16[2,32,8,256]{3,2,0,1:T(8,128)(2,1)} %copy.156) | copy-start | bytes 786436
  145.9 53.1 %collective-permute-start.4 = (bf16[16,1,256]{2,0,1:T(8,128)(2,1)S(1)}, bf16[16,1,256]{2,0,1:T(8,128)(2,1)S(1)}, u32[]{:S(2)}, u32[]{:S(2)}) collective-permute-start(bf16[16,1,256]{2,0,1:T(8,128)(2,1)S(1)} %get-tuple-element.19), channel_id=1, source_target_pairs={{0,4},{4,8},{8,12},{12,16},{16,20},{20,24},{24,28},{28,32},{32,36}... | collective-permute-start | bytes 24584 | tf_op jit(solution)/shard_map/ppermute | solution.py:15
  203.3 94.9 %all-gather.15.cloned.1.call-start = ((), (), s32[]{:S(2)}) async-start(), calls=%async_computation.5 | async-start | bytes 2621440 | tf_op jit(solution)/shard_map/all_gather | solution.py:55
  204.1 6.2 %collective-permute-start.7 = (bf16[16,1,256]{2,0,1:T(8,128)(2,1)S(1)}, bf16[16,1,256]{2,0,1:T(8,128)(2,1)S(1)}, u32[]{:S(2)}, u32[]{:S(2)}) collective-permute-start(bf16[16,1,256]{2,0,1:T(8,128)(2,1)S(1)} %get-tuple-element.18), channel_id=1, source_target_pairs={{4,0},{8,4},{12,8},{16,12},{20,16},{24,20},{28,24},{32,28},{36,32}... | collective-permute-start | bytes 24584 | tf_op jit(solution)/shard_map/ppermute | solution.py:18
  210.3 53.1 %copy-start.7 = (bf16[2,32,8,256]{3,2,0,1:T(8,128)(2,1)S(1)}, bf16[2,32,8,256]{3,2,0,1:T(8,128)(2,1)}, u32[]{:S(2)}) copy-start(bf16[2,32,8,256]{3,2,0,1:T(8,128)(2,1)} %copy.155) | copy-start | bytes 786436
  210.3 53.1 %collective-permute-start.6 = (bf16[16,1,256]{2,0,1:T(8,128)(2,1)S(1)}, bf16[16,1,256]{2,0,1:T(8,128)(2,1)S(1)}, u32[]{:S(2)}, u32[]{:S(2)}) collective-permute-start(bf16[16,1,256]{2,0,1:T(8,128)(2,1)S(1)} %get-tuple-element.17), channel_id=1, source_target_pairs={{0,4},{4,8},{8,12},{12,16},{16,20},{20,24},{24,28},{28,32},{32,36}... | collective-permute-start | bytes 24584 | tf_op jit(solution)/shard_map/ppermute | solution.py:15
  267.7 85.7 %all-gather.17.cloned.1.call-start = ((), (), s32[]{:S(2)}) async-start(), calls=%async_computation.6 | async-start | bytes 8650752 | tf_op jit(solution)/shard_map/all_gather | solution.py:42
  269.2 6.3 %collective-permute-start.9 = (bf16[16,1,256]{2,0,1:T(8,128)(2,1)S(1)}, bf16[16,1,256]{2,0,1:T(8,128)(2,1)S(1)}, u32[]{:S(2)}, u32[]{:S(2)}) collective-permute-start(bf16[16,1,256]{2,0,1:T(8,128)(2,1)S(1)} %get-tuple-element.16), channel_id=1, source_target_pairs={{4,0},{8,4},{12,8},{16,12},{20,16},{24,20},{28,24},{32,28},{36,32}... | collective-permute-start | bytes 24584 | tf_op jit(solution)/shard_map/ppermute | solution.py:18
  275.4 22.8 %copy-start.1 = (f32[16,8192]{1,0:T(8,128)S(1)}, f32[16,8192]{1,0:T(8,128)}, u32[]{:S(2)}) copy-start(f32[16,8192]{1,0:T(8,128)} %get-tuple-element.6) | copy-start | bytes 1572868
  275.4 85.3 %copy-start.3 = (bf16[2,32,8,256]{3,2,0,1:T(8,128)(2,1)S(1)}, bf16[2,32,8,256]{3,2,0,1:T(8,128)(2,1)}, u32[]{:S(2)}) copy-start(bf16[2,32,8,256]{3,2,0,1:T(8,128)(2,1)} %copy.154) | copy-start | bytes 786436
  275.4 85.3 %collective-permute-start.8 = (bf16[16,1,256]{2,0,1:T(8,128)(2,1)S(1)}, bf16[16,1,256]{2,0,1:T(8,128)(2,1)S(1)}, u32[]{:S(2)}, u32[]{:S(2)}) collective-permute-start(bf16[16,1,256]{2,0,1:T(8,128)(2,1)S(1)} %get-tuple-element.15), channel_id=1, source_target_pairs={{0,4},{4,8},{8,12},{12,16},{16,20},{20,24},{24,28},{28,32},{32,36}... | collective-permute-start | bytes 24584 | tf_op jit(solution)/shard_map/ppermute | solution.py:15
  360.7 3.6 copy-start
  493.4 17.2 %all-to-all-start = ((f32[4,1,1024]{2,1,0:T(1,128)}), f32[4,1,1024]{2,1,0:T(1,128)S(1)}, u32[]{:S(2)}, u32[]{:S(2)}) async-start(f32[4,1,1024]{2,1,0:T(1,128)} %reshape.116), calls=%async_computation | async-start | bytes 32768 | tf_op jit(solution)/shard_map/all_to_all | solution.py:62
  (1 other events, 3.6 us)
Sparse Core Ops, SparseCore 0:
  10.8 55.4 all-gather.6
  74.7 52.5 all-gather.8
  139.1 52.5 all-gather.10
  203.4 52.5 all-gather.12
  267.8 30.2 all-gather.14
  300.3 53.0 all-gather.16
